TPU v7x, 32 devices: a whole 2x2x4 slice. The times are simulated.
32 devices in a mesh: member: 2 (over x), lon: 8 (over z, y), lat: 2 (over core).
Axes of the slice: x: 2, y: 2, z: 4, core: 2. Of those that a mesh axis runs over, the one named last changes fastest.
Arguments:
- forcing: float32 [4, 192, 1024], P('member', 'lat', 'lon'), parts along dimension 0, may hold values from -8 to 8
- coeffs: float32 [8, 2, 192, 1024], P(None, None, 'lat', 'lon'), may hold values from 0.02 to 0.6
- sea_mask: int32 [2, 192, 1024], P(None, 'lat', 'lon'), may hold values 0 or 1
- fold_pair: int32 [1024], replicated, may hold values from 0 to 1023, as said below
- norm_scale: float32 [2, 192, 1024], P(None, 'lat', 'lon'), may hold values from 0.5 to 2
Outputs:
- adjoint_field: float32 [4, 192, 1024], P('member', 'lat', 'lon'), parts along dimension 0
There are 2 independent parts, one for each index of `member`. A program takes and returns all parts, laid end to end along the dimension named above; an argument that names none is the same for every part. Nothing has to cross between parts.
Inputs may be any that keep to these rules, and one draw needn't show every extreme that they name: fold_pair is the tripolar fold's mirror with staggering: fold_pair[i] = (1023 - i + o_i) mod 1024, with each column's own offset o_i of 0, 1 or 2.
All inputs are finite; a program needn't handle non-finite values. No bound on the sum of `sea_mask` on one device may be relied on, other than what follows from the above.
Results may differ from a plain program's by a relative error of at most 0.00002.
Values sent between devices are 32-bit elements; how exact they have to be, the bound alone decides.
A program may use at most 64 MiB of HBM per device.

v0:
```python
import jax
import jax.numpy as jnp
from jax import lax
from jax.sharding import PartitionSpec as P

STEPS = 2
ITERS = 4


OFFSETS = ((1, 0), (-1, 0), (0, 1), (0, -1), (1, 1), (1, -1), (-1, 1), (-1, -1))
CENTRE_VALUE = 1.05
HALF_WIDTH = 0.9


def extended(value, sides, width, wrap):
    for axis, dim in sides:
        size, length = (lax.axis_size(axis), value.shape[dim])
        up = [(i, (i + 1) % size) for i in range(size if wrap else size - 1)]
        down = [(j, i) for i, j in up]
        last = lax.slice_in_dim(value, length - width, length, axis=dim)
        first = lax.slice_in_dim(value, 0, width, axis=dim)
        before = lax.ppermute(last, axis, up)
        after = lax.ppermute(first, axis, down)
        value = jnp.concatenate([before, value, after], axis=dim)
    return value


def extend_rims(stack):
    beside_all = extended(stack, (("lon", 3),), 1, True)
    return extended(beside_all, (("lat", 2),), 1, False)


def fold_term(top_row, fold_pair):
    columns = top_row.shape[1]
    start = lax.axis_index("lon") * columns
    mine = lax.dynamic_slice_in_dim(fold_pair, start, columns, 0)
    placed = (
        jnp.zeros((top_row.shape[0], columns * lax.axis_size("lon")), top_row.dtype)
        .at[:, mine]
        .add(top_row)
    )
    return lax.psum_scatter(placed, "lon", scatter_dimension=1, tiled=True)


def spread_field(field, coeffs, fold_pair):
    rows = field.shape[1]
    columns = field.shape[2]
    total = jnp.zeros_like(field)
    wide = extend_rims(coeffs * field[None])
    for index_dir, (shift_lat, shift_lon) in enumerate(OFFSETS):
        total = (
            total
            + wide[
                index_dir,
                :,
                1 - shift_lat : 1 - shift_lat + rows,
                1 - shift_lon : 1 - shift_lon + columns,
            ]
        )
    top_row = coeffs[0, :, -1, :] * field[:, -1, :]
    across = fold_term(top_row, fold_pair)
    is_top = lax.axis_index("lat") == lax.axis_size("lat") - 1
    return total.at[:, -1, :].add(jnp.where(is_top, across, 0.0))


def chebyshev(rhs, apply_op, precond):
    sigma_ratio = CENTRE_VALUE / HALF_WIDTH
    ratio_now = 1.0 / sigma_ratio
    residual = rhs
    update = precond * residual / CENTRE_VALUE
    iterate = update
    for sweep in range(ITERS):
        residual = residual - apply_op(update)
        ratio_next = 1.0 / (2.0 * sigma_ratio - ratio_now)
        update = ratio_next * ratio_now * update + 2.0 * ratio_next / HALF_WIDTH * (
            precond * residual
        )
        iterate = iterate + update
        ratio_now = ratio_next
    return iterate


def body(forcing, coeffs, sea_mask, fold_pair, norm_scale):
    sea = sea_mask.astype(jnp.float32)
    diag_sum = coeffs[0]
    for index_dir in range(1, 8):
        diag_sum = diag_sum + coeffs[index_dir]
    precond = 1.0 / (1.0 + diag_sum)

    def apply_op(field):
        return sea * ((1.0 + diag_sum) * field - spread_field(field, coeffs, fold_pair))

    state = sea * norm_scale * forcing
    for step in range(STEPS):
        state = chebyshev(state, apply_op, precond)
    return norm_scale * state


def solution(mesh):
    placed = (
        P("member", "lat", "lon"),
        P(None, None, "lat", "lon"),
        P(None, "lat", "lon"),
        P(),
        P(None, "lat", "lon"),
    )
    return jax.shard_map(
        body, mesh=mesh, in_specs=placed, out_specs=P("member", "lat", "lon"), check_vma=False
    )
```

profile of v0, /device:TPU:1, one launch (start us, length us, event | category | flops | bytes accessed | tf_op | source)
XLA Modules:
  0.0 563.0 jit_solution(2672549348795266392)
XLA Ops:
  10.1 2.1 collective-permute-start
  12.3 3.1 collective-permute-start.1
  16.3 1.8 scatter_custom_fusion
  19.9 1.9 copy.684
  23.1 1.9 copy.685
  25.0 3.0 collective-permute-start.3
  32.8 44.5 %reduce-scatter.25.cloned.1.call-done = f32[128,2]{1,0:T(8,128)} async-done(((f32[1024,2]{1,0:T(8,128)}), f32[128,2]{1,0:T(8,128)}) %reduce-scatter.25.cloned.1.call-update) | async-done | bytes 1040
  80.2 3.1 collective-permute-start.5
  83.4 2.0 scatter_custom_fusion.1
  88.5 2.5 copy.689
  92.2 2.5 copy.690
  94.7 6.2 %collective-permute-start.7 = (f32[8,2,1,130]{3,0,2,1:T(8,128)}, f32[8,2,1,130]{3,0,2,1:T(8,128)}, u32[]{:S(2)}, u32[]{:S(2)}) collective-permute-start(f32[8,2,1,130]{3,0,2,1:T(8,128)} %copy.690), channel_id=1, source_target_pairs={{1,0},{3,2},{5,4},{7,6},{9,8},{11,10},{13,12},{15,14},{17,16},{19,... | collective-permute-start | bytes 24968 | tf_op jit(solution)/shard_map/ppermute | solution.py:23
  107.9 37.4 %reduce-scatter.27.cloned.1.call-done = f32[128,2]{1,0:T(8,128)} async-done(((f32[1024,2]{1,0:T(8,128)}), f32[128,2]{1,0:T(8,128)}) %reduce-scatter.27.cloned.1.call-update) | async-done | bytes 1040
  148.5 3.2 collective-permute-start.9
  151.8 2.0 scatter_custom_fusion.2
  156.8 2.5 copy.693
  160.6 2.5 copy.694
  163.1 6.2 %collective-permute-start.11 = (f32[8,2,1,130]{3,0,2,1:T(8,128)}, f32[8,2,1,130]{3,0,2,1:T(8,128)}, u32[]{:S(2)}, u32[]{:S(2)}) collective-permute-start(f32[8,2,1,130]{3,0,2,1:T(8,128)} %copy.694), channel_id=1, source_target_pairs={{1,0},{3,2},{5,4},{7,6},{9,8},{11,10},{13,12},{15,14},{17,16},{19,... | collective-permute-start | bytes 24968 | tf_op jit(solution)/shard_map/ppermute | solution.py:23
  176.2 37.4 %reduce-scatter.29.cloned.1.call-done = f32[128,2]{1,0:T(8,128)} async-done(((f32[1024,2]{1,0:T(8,128)}), f32[128,2]{1,0:T(8,128)}) %reduce-scatter.29.cloned.1.call-update) | async-done | bytes 1040
  216.4 3.2 collective-permute-start.13
  219.7 2.0 scatter_custom_fusion.3
  224.8 2.5 copy.697
  228.5 2.5 copy.698
  231.0 6.2 %collective-permute-start.15 = (f32[8,2,1,130]{3,0,2,1:T(8,128)}, f32[8,2,1,130]{3,0,2,1:T(8,128)}, u32[]{:S(2)}, u32[]{:S(2)}) collective-permute-start(f32[8,2,1,130]{3,0,2,1:T(8,128)} %copy.698), channel_id=1, source_target_pairs={{1,0},{3,2},{5,4},{7,6},{9,8},{11,10},{13,12},{15,14},{17,16},{19,... | collective-permute-start | bytes 24968 | tf_op jit(solution)/shard_map/ppermute | solution.py:23
  244.2 37.4 %reduce-scatter.31.cloned.1.call-done = f32[128,2]{1,0:T(8,128)} async-done(((f32[1024,2]{1,0:T(8,128)}), f32[128,2]{1,0:T(8,128)}) %reduce-scatter.31.cloned.1.call-update) | async-done | bytes 1040
  284.9 3.1 collective-permute-start.17
  288.2 2.0 scatter_custom_fusion.4
  292.0 1.9 copy.701
  295.1 1.9 copy.702
  297.0 5.0 collective-permute-start.19
  306.8 43.3 %reduce-scatter.33.cloned.1.call-done = f32[128,2]{1,0:T(8,128)} async-done(((f32[1024,2]{1,0:T(8,128)}), f32[128,2]{1,0:T(8,128)}) %reduce-scatter.33.cloned.1.call-update) | async-done | bytes 1040
  352.9 3.2 collective-permute-start.21
  356.2 2.0 scatter_custom_fusion.5
  360.0 1.9 copy.705
  363.4 1.9 copy.706
  365.2 5.0 collective-permute-start.23
  375.0 43.0 %reduce-scatter.35.cloned.1.call-done = f32[128,2]{1,0:T(8,128)} async-done(((f32[1024,2]{1,0:T(8,128)}), f32[128,2]{1,0:T(8,128)}) %reduce-scatter.35.cloned.1.call-update) | async-done | bytes 1040
  421.3 3.1 collective-permute-start.25
  424.6 2.0 scatter_custom_fusion.6
  429.6 2.5 copy.709
  433.4 2.5 copy.710
  435.9 6.2 %collective-permute-start.27 = (f32[8,2,1,130]{3,0,2,1:T(8,128)}, f32[8,2,1,130]{3,0,2,1:T(8,128)}, u32[]{:S(2)}, u32[]{:S(2)}) collective-permute-start(f32[8,2,1,130]{3,0,2,1:T(8,128)} %copy.710), channel_id=1, source_target_pairs={{1,0},{3,2},{5,4},{7,6},{9,8},{11,10},{13,12},{15,14},{17,16},{19,... | collective-permute-start | bytes 24968 | tf_op jit(solution)/shard_map/ppermute | solution.py:23
  449.0 37.4 %reduce-scatter.37.cloned.1.call-done = f32[128,2]{1,0:T(8,128)} async-done(((f32[1024,2]{1,0:T(8,128)}), f32[128,2]{1,0:T(8,128)}) %reduce-scatter.37.cloned.1.call-update) | async-done | bytes 1040
  489.1 3.2 collective-permute-start.29
  492.4 1.9 scatter_custom_fusion.7
  495.8 1.9 copy.713
  499.6 5.0 collective-permute-start.31
  506.9 47.4 %reduce-scatter.39.cloned.1.call-done = f32[128,2]{1,0:T(8,128)} async-done(((f32[1024,2]{1,0:T(8,128)}), f32[128,2]{1,0:T(8,128)}) %reduce-scatter.39.cloned.1.call-update) | async-done | bytes 1040
  (316 shorter events, 101.8 us)
Async XLA Ops:
  6.5 70.7 %reduce-scatter.25.cloned.1.call-start = ((), (), s32[]{:S(2)}) async-start(), calls=%async_computation.8 | async-start | bytes 589824
  10.1 8.0 %collective-permute-start = (f32[8,2,96,1]{2,0,3,1:T(8,128)S(1)}, f32[8,2,96,1]{2,0,3,1:T(8,128)S(1)}, u32[]{:S(2)}, u32[]{:S(2)}) collective-permute-start(f32[8,2,96,1]{2,0,3,1:T(8,128)S(1)} %get-tuple-element.156), channel_id=1, source_target_pairs={{0,2},{2,4},{4,6},{6,8},{8,10},{10,12},{12,14},{14,0},{1,3},{3,5},... | collective-permute-start | bytes 18440 | tf_op jit(solution)/shard_map/ppermute | solution.py:22
  12.3 5.9 %collective-permute-start.1 = (f32[8,2,96,1]{2,0,3,1:T(8,128)S(1)}, f32[8,2,96,1]{2,0,3,1:T(8,128)S(1)}, u32[]{:S(2)}, u32[]{:S(2)}) collective-permute-start(f32[8,2,96,1]{2,0,3,1:T(8,128)S(1)} %get-tuple-element.157), channel_id=1, source_target_pairs={{2,0},{4,2},{6,4},{8,6},{10,8},{12,10},{14,12},{0,14},{3,1},{5,3},... | collective-permute-start | bytes 18440 | tf_op jit(solution)/shard_map/ppermute | solution.py:23
  18.1 127.2 %reduce-scatter.27.cloned.1.call-start = ((), (), s32[]{:S(2)}) async-start(), calls=%async_computation.9 | async-start | bytes 589824
  21.8 9.2 %collective-permute-start.2 = (f32[8,2,1,130]{3,0,2,1:T(8,128)S(1)}, f32[8,2,1,130]{3,0,2,1:T(8,128)S(1)}, u32[]{:S(2)}, u32[]{:S(2)}) collective-permute-start(f32[8,2,1,130]{3,0,2,1:T(8,128)S(1)} %copy.684), channel_id=1, source_target_pairs={{0,1},{2,3},{4,5},{6,7},{8,9},{10,11},{12,13},{14,15},{16,17},{18,... | collective-permute-start | bytes 24968 | tf_op jit(solution)/shard_map/ppermute | solution.py:22
  25.0 6.0 %collective-permute-start.3 = (f32[8,2,1,130]{3,0,2,1:T(8,128)S(1)}, f32[8,2,1,130]{3,0,2,1:T(8,128)S(1)}, u32[]{:S(2)}, u32[]{:S(2)}) collective-permute-start(f32[8,2,1,130]{3,0,2,1:T(8,128)S(1)} %copy.685), channel_id=1, source_target_pairs={{1,0},{3,2},{5,4},{7,6},{9,8},{11,10},{13,12},{15,14},{17,16},{19,... | collective-permute-start | bytes 24968 | tf_op jit(solution)/shard_map/ppermute | solution.py:23
  30.9 47.3 %copy-start.4 = (f32[2,96,128]{2,0,1:T(2,128)S(1)}, f32[2,96,128]{2,0,1:T(2,128)}, u32[]{:S(2)}) copy-start(f32[2,96,128]{2,0,1:T(2,128)} %get-tuple-element.109) | copy-start | bytes 294916
  79.1 6.4 %collective-permute-start.4 = (f32[8,2,96,1]{2,0,3,1:T(8,128)S(1)}, f32[8,2,96,1]{2,0,3,1:T(8,128)S(1)}, u32[]{:S(2)}, u32[]{:S(2)}) collective-permute-start(f32[8,2,96,1]{2,0,3,1:T(8,128)S(1)} %get-tuple-element.152), channel_id=1, source_target_pairs={{0,2},{2,4},{4,6},{6,8},{8,10},{10,12},{12,14},{14,0},{1,3},{3,5},... | collective-permute-start | bytes 18440 | tf_op jit(solution)/shard_map/ppermute | solution.py:22
  80.2 5.9 %collective-permute-start.5 = (f32[8,2,96,1]{2,0,3,1:T(8,128)S(1)}, f32[8,2,96,1]{2,0,3,1:T(8,128)}, u32[]{:S(2)}, u32[]{:S(2)}) collective-permute-start(f32[8,2,96,1]{2,0,3,1:T(8,128)S(1)} %get-tuple-element.153), channel_id=1, source_target_pairs={{2,0},{4,2},{6,4},{8,6},{10,8},{12,10},{14,12},{0,14},{3,1},{5,3},... | collective-permute-start | bytes 18440 | tf_op jit(solution)/shard_map/ppermute | solution.py:23
  85.4 128.2 %reduce-scatter.29.cloned.1.call-start = ((), (), s32[]{:S(2)}) async-start(), calls=%async_computation.10 | async-start | bytes 589824
  91.0 13.6 %collective-permute-start.6 = (f32[8,2,1,130]{3,0,2,1:T(8,128)}, f32[8,2,1,130]{3,0,2,1:T(8,128)}, u32[]{:S(2)}, u32[]{:S(2)}) collective-permute-start(f32[8,2,1,130]{3,0,2,1:T(8,128)} %copy.689), channel_id=1, source_target_pairs={{0,1},{2,3},{4,5},{6,7},{8,9},{10,11},{12,13},{14,15},{16,17},{18,... | collective-permute-start | bytes 24968 | tf_op jit(solution)/shard_map/ppermute | solution.py:22
  94.7 10.6 %collective-permute-start.7 = (f32[8,2,1,130]{3,0,2,1:T(8,128)}, f32[8,2,1,130]{3,0,2,1:T(8,128)}, u32[]{:S(2)}, u32[]{:S(2)}) collective-permute-start(f32[8,2,1,130]{3,0,2,1:T(8,128)} %copy.690), channel_id=1, source_target_pairs={{1,0},{3,2},{5,4},{7,6},{9,8},{11,10},{13,12},{15,14},{17,16},{19,... | collective-permute-start | bytes 24968 | tf_op jit(solution)/shard_map/ppermute | solution.py:23
  147.4 6.4 %collective-permute-start.8 = (f32[8,2,96,1]{2,0,3,1:T(8,128)S(1)}, f32[8,2,96,1]{2,0,3,1:T(8,128)S(1)}, u32[]{:S(2)}, u32[]{:S(2)}) collective-permute-start(f32[8,2,96,1]{2,0,3,1:T(8,128)S(1)} %get-tuple-element.148), channel_id=1, source_target_pairs={{0,2},{2,4},{4,6},{6,8},{8,10},{10,12},{12,14},{14,0},{1,3},{3,5},... | collective-permute-start | bytes 18440 | tf_op jit(solution)/shard_map/ppermute | solution.py:22
  148.5 5.9 %collective-permute-start.9 = (f32[8,2,96,1]{2,0,3,1:T(8,128)S(1)}, f32[8,2,96,1]{2,0,3,1:T(8,128)}, u32[]{:S(2)}, u32[]{:S(2)}) collective-permute-start(f32[8,2,96,1]{2,0,3,1:T(8,128)S(1)} %get-tuple-element.149), channel_id=1, source_target_pairs={{2,0},{4,2},{6,4},{8,6},{10,8},{12,10},{14,12},{0,14},{3,1},{5,3},... | collective-permute-start | bytes 18440 | tf_op jit(solution)/shard_map/ppermute | solution.py:23
  153.7 127.9 %reduce-scatter.31.cloned.1.call-start = ((), (), s32[]{:S(2)}) async-start(), calls=%async_computation.11 | async-start | bytes 589824
  159.3 13.6 %collective-permute-start.10 = (f32[8,2,1,130]{3,0,2,1:T(8,128)}, f32[8,2,1,130]{3,0,2,1:T(8,128)}, u32[]{:S(2)}, u32[]{:S(2)}) collective-permute-start(f32[8,2,1,130]{3,0,2,1:T(8,128)} %copy.693), channel_id=1, source_target_pairs={{0,1},{2,3},{4,5},{6,7},{8,9},{10,11},{12,13},{14,15},{16,17},{18,... | collective-permute-start | bytes 24968 | tf_op jit(solution)/shard_map/ppermute | solution.py:22
  163.1 10.6 %collective-permute-start.11 = (f32[8,2,1,130]{3,0,2,1:T(8,128)}, f32[8,2,1,130]{3,0,2,1:T(8,128)}, u32[]{:S(2)}, u32[]{:S(2)}) collective-permute-start(f32[8,2,1,130]{3,0,2,1:T(8,128)} %copy.694), channel_id=1, source_target_pairs={{1,0},{3,2},{5,4},{7,6},{9,8},{11,10},{13,12},{15,14},{17,16},{19,... | collective-permute-start | bytes 24968 | tf_op jit(solution)/shard_map/ppermute | solution.py:23
  215.4 6.4 %collective-permute-start.12 = (f32[8,2,96,1]{2,0,3,1:T(8,128)S(1)}, f32[8,2,96,1]{2,0,3,1:T(8,128)S(1)}, u32[]{:S(2)}, u32[]{:S(2)}) collective-permute-start(f32[8,2,96,1]{2,0,3,1:T(8,128)S(1)} %get-tuple-element.144), channel_id=1, source_target_pairs={{0,2},{2,4},{4,6},{6,8},{8,10},{10,12},{12,14},{14,0},{1,3},{3,5},... | collective-permute-start | bytes 18440 | tf_op jit(solution)/shard_map/ppermute | solution.py:22
  216.4 5.9 %collective-permute-start.13 = (f32[8,2,96,1]{2,0,3,1:T(8,128)S(1)}, f32[8,2,96,1]{2,0,3,1:T(8,128)}, u32[]{:S(2)}, u32[]{:S(2)}) collective-permute-start(f32[8,2,96,1]{2,0,3,1:T(8,128)S(1)} %get-tuple-element.145), channel_id=1, source_target_pairs={{2,0},{4,2},{6,4},{8,6},{10,8},{12,10},{14,12},{0,14},{3,1},{5,3},... | collective-permute-start | bytes 18440 | tf_op jit(solution)/shard_map/ppermute | solution.py:23
  221.7 128.4 %reduce-scatter.33.cloned.1.call-start = ((), (), s32[]{:S(2)}) async-start(), calls=%async_computation.12 | async-start | bytes 589824
  227.3 13.6 %collective-permute-start.14 = (f32[8,2,1,130]{3,0,2,1:T(8,128)}, f32[8,2,1,130]{3,0,2,1:T(8,128)}, u32[]{:S(2)}, u32[]{:S(2)}) collective-permute-start(f32[8,2,1,130]{3,0,2,1:T(8,128)} %copy.697), channel_id=1, source_target_pairs={{0,1},{2,3},{4,5},{6,7},{8,9},{10,11},{12,13},{14,15},{16,17},{18,... | collective-permute-start | bytes 24968 | tf_op jit(solution)/shard_map/ppermute | solution.py:22
  231.0 10.7 %collective-permute-start.15 = (f32[8,2,1,130]{3,0,2,1:T(8,128)}, f32[8,2,1,130]{3,0,2,1:T(8,128)}, u32[]{:S(2)}, u32[]{:S(2)}) collective-permute-start(f32[8,2,1,130]{3,0,2,1:T(8,128)} %copy.698), channel_id=1, source_target_pairs={{1,0},{3,2},{5,4},{7,6},{9,8},{11,10},{13,12},{15,14},{17,16},{19,... | collective-permute-start | bytes 24968 | tf_op jit(solution)/shard_map/ppermute | solution.py:23
  283.9 6.4 %collective-permute-start.16 = (f32[8,2,96,1]{2,0,3,1:T(8,128)S(1)}, f32[8,2,96,1]{2,0,3,1:T(8,128)S(1)}, u32[]{:S(2)}, u32[]{:S(2)}) collective-permute-start(f32[8,2,96,1]{2,0,3,1:T(8,128)S(1)} %get-tuple-element.140), channel_id=1, source_target_pairs={{0,2},{2,4},{4,6},{6,8},{8,10},{10,12},{12,14},{14,0},{1,3},{3,5},... | collective-permute-start | bytes 18440 | tf_op jit(solution)/shard_map/ppermute | solution.py:22
  284.9 5.3 collective-permute-start.17
  290.2 127.9 %reduce-scatter.35.cloned.1.call-start = ((), (), s32[]{:S(2)}) async-start(), calls=%async_computation.13 | async-start | bytes 589824
  293.8 11.2 %collective-permute-start.18 = (f32[8,2,1,130]{3,0,2,1:T(8,128)S(1)}, f32[8,2,1,130]{3,0,2,1:T(8,128)S(1)}, u32[]{:S(2)}, u32[]{:S(2)}) collective-permute-start(f32[8,2,1,130]{3,0,2,1:T(8,128)S(1)} %copy.701), channel_id=1, source_target_pairs={{0,1},{2,3},{4,5},{6,7},{8,9},{10,11},{12,13},{14,15},{16,17},{18,... | collective-permute-start | bytes 24968 | tf_op jit(solution)/shard_map/ppermute | solution.py:22
  297.0 8.0 %collective-permute-start.19 = (f32[8,2,1,130]{3,0,2,1:T(8,128)S(1)}, f32[8,2,1,130]{3,0,2,1:T(8,128)S(1)}, u32[]{:S(2)}, u32[]{:S(2)}) collective-permute-start(f32[8,2,1,130]{3,0,2,1:T(8,128)S(1)} %copy.702), channel_id=1, source_target_pairs={{1,0},{3,2},{5,4},{7,6},{9,8},{11,10},{13,12},{15,14},{17,16},{19,... | collective-permute-start | bytes 24968 | tf_op jit(solution)/shard_map/ppermute | solution.py:23
  305.0 46.0 %copy-start.21 = (f32[2,96,128]{2,0,1:T(2,128)S(1)}, f32[2,96,128]{2,0,1:T(2,128)}, u32[]{:S(2)}) copy-start(f32[2,96,128]{2,0,1:T(2,128)} %get-tuple-element.105) | copy-start | bytes 294916
  351.9 6.4 %collective-permute-start.20 = (f32[8,2,96,1]{2,0,3,1:T(8,128)S(1)}, f32[8,2,96,1]{2,0,3,1:T(8,128)S(1)}, u32[]{:S(2)}, u32[]{:S(2)}) collective-permute-start(f32[8,2,96,1]{2,0,3,1:T(8,128)S(1)} %get-tuple-element.136), channel_id=1, source_target_pairs={{0,2},{2,4},{4,6},{6,8},{8,10},{10,12},{12,14},{14,0},{1,3},{3,5},... | collective-permute-start | bytes 18440 | tf_op jit(solution)/shard_map/ppermute | solution.py:22
  352.9 5.3 collective-permute-start.21
  358.2 128.2 %reduce-scatter.37.cloned.1.call-start = ((), (), s32[]{:S(2)}) async-start(), calls=%async_computation.14 | async-start | bytes 589824
  361.9 11.3 %collective-permute-start.22 = (f32[8,2,1,130]{3,0,2,1:T(8,128)S(1)}, f32[8,2,1,130]{3,0,2,1:T(8,128)S(1)}, u32[]{:S(2)}, u32[]{:S(2)}) collective-permute-start(f32[8,2,1,130]{3,0,2,1:T(8,128)S(1)} %copy.705), channel_id=1, source_target_pairs={{0,1},{2,3},{4,5},{6,7},{8,9},{10,11},{12,13},{14,15},{16,17},{18,... | collective-permute-start | bytes 24968 | tf_op jit(solution)/shard_map/ppermute | solution.py:22
  365.2 7.9 %collective-permute-start.23 = (f32[8,2,1,130]{3,0,2,1:T(8,128)S(1)}, f32[8,2,1,130]{3,0,2,1:T(8,128)S(1)}, u32[]{:S(2)}, u32[]{:S(2)}) collective-permute-start(f32[8,2,1,130]{3,0,2,1:T(8,128)S(1)} %copy.706), channel_id=1, source_target_pairs={{1,0},{3,2},{5,4},{7,6},{9,8},{11,10},{13,12},{15,14},{17,16},{19,... | collective-permute-start | bytes 24968 | tf_op jit(solution)/shard_map/ppermute | solution.py:23
  420.0 67.3 %copy-start.2 = (f32[2,96,128]{2,0,1:T(2,128)}, f32[2,96,128]{2,0,1:T(2,128)S(1)}, u32[]{:S(2)}) copy-start(f32[2,96,128]{2,0,1:T(2,128)S(1)} %get-tuple-element.102) | copy-start | bytes 294916
  420.2 6.4 %collective-permute-start.24 = (f32[8,2,96,1]{2,0,3,1:T(8,128)S(1)}, f32[8,2,96,1]{2,0,3,1:T(8,128)S(1)}, u32[]{:S(2)}, u32[]{:S(2)}) collective-permute-start(f32[8,2,96,1]{2,0,3,1:T(8,128)S(1)} %get-tuple-element.132), channel_id=1, source_target_pairs={{0,2},{2,4},{4,6},{6,8},{8,10},{10,12},{12,14},{14,0},{1,3},{3,5},... | collective-permute-start | bytes 18440 | tf_op jit(solution)/shard_map/ppermute | solution.py:22
  421.3 5.9 %collective-permute-start.25 = (f32[8,2,96,1]{2,0,3,1:T(8,128)S(1)}, f32[8,2,96,1]{2,0,3,1:T(8,128)}, u32[]{:S(2)}, u32[]{:S(2)}) collective-permute-start(f32[8,2,96,1]{2,0,3,1:T(8,128)S(1)} %get-tuple-element.133), channel_id=1, source_target_pairs={{2,0},{4,2},{6,4},{8,6},{10,8},{12,10},{14,12},{0,14},{3,1},{5,3},... | collective-permute-start | bytes 18440 | tf_op jit(solution)/shard_map/ppermute | solution.py:23
  426.6 127.7 %reduce-scatter.39.cloned.1.call-start = ((), (), s32[]{:S(2)}) async-start(), calls=%async_computation.15 | async-start | bytes 589824
  432.1 13.6 %collective-permute-start.26 = (f32[8,2,1,130]{3,0,2,1:T(8,128)}, f32[8,2,1,130]{3,0,2,1:T(8,128)}, u32[]{:S(2)}, u32[]{:S(2)}) collective-permute-start(f32[8,2,1,130]{3,0,2,1:T(8,128)} %copy.709), channel_id=1, source_target_pairs={{0,1},{2,3},{4,5},{6,7},{8,9},{10,11},{12,13},{14,15},{16,17},{18,... | collective-permute-start | bytes 24968 | tf_op jit(solution)/shard_map/ppermute | solution.py:22
  435.9 10.6 %collective-permute-start.27 = (f32[8,2,1,130]{3,0,2,1:T(8,128)}, f32[8,2,1,130]{3,0,2,1:T(8,128)}, u32[]{:S(2)}, u32[]{:S(2)}) collective-permute-start(f32[8,2,1,130]{3,0,2,1:T(8,128)} %copy.710), channel_id=1, source_target_pairs={{1,0},{3,2},{5,4},{7,6},{9,8},{11,10},{13,12},{15,14},{17,16},{19,... | collective-permute-start | bytes 24968 | tf_op jit(solution)/shard_map/ppermute | solution.py:23
  488.1 6.3 %collective-permute-start.28 = (f32[8,2,96,1]{2,0,3,1:T(8,128)S(1)}, f32[8,2,96,1]{2,0,3,1:T(8,128)S(1)}, u32[]{:S(2)}, u32[]{:S(2)}) collective-permute-start(f32[8,2,96,1]{2,0,3,1:T(8,128)S(1)} %get-tuple-element.128), channel_id=1, source_target_pairs={{0,2},{2,4},{4,6},{6,8},{8,10},{10,12},{12,14},{14,0},{1,3},{3,5},... | collective-permute-start | bytes 18440 | tf_op jit(solution)/shard_map/ppermute | solution.py:22
  489.1 5.3 collective-permute-start.29
  497.7 8.6 %collective-permute-start.30 = (f32[8,2,1,130]{3,0,2,1:T(8,128)S(1)}, f32[8,2,1,130]{3,0,2,1:T(8,128)S(1)}, u32[]{:S(2)}, u32[]{:S(2)}) collective-permute-start(f32[8,2,1,130]{3,0,2,1:T(8,128)S(1)} %copy.713), channel_id=1, source_target_pairs={{0,1},{2,3},{4,5},{6,7},{8,9},{10,11},{12,13},{14,15},{16,17},{18,... | collective-permute-start | bytes 24968 | tf_op jit(solution)/shard_map/ppermute | solution.py:22
  499.6 6.7 %collective-permute-start.31 = (f32[8,2,1,130]{3,0,2,1:T(8,128)S(1)}, f32[8,2,1,130]{3,0,2,1:T(8,128)S(1)}, u32[]{:S(2)}, u32[]{:S(2)}) collective-permute-start(f32[8,2,1,130]{3,0,2,1:T(8,128)S(1)} %copy.714), channel_id=1, source_target_pairs={{1,0},{3,2},{5,4},{7,6},{9,8},{11,10},{13,12},{15,14},{17,16},{19,... | collective-permute-start | bytes 24968 | tf_op jit(solution)/shard_map/ppermute | solution.py:23
  506.3 48.9 %copy-start.3 = (f32[2,96,128]{2,0,1:T(2,128)S(1)}, f32[2,96,128]{2,0,1:T(2,128)}, u32[]{:S(2)}) copy-start(f32[2,96,128]{2,0,1:T(2,128)} %copy-done.2) | copy-start | bytes 294916
  506.3 48.9 %copy-start.12 = (f32[2,96,128]{2,0,1:T(2,128)S(1)}, f32[2,96,128]{2,0,1:T(2,128)}, u32[]{:S(2)}) copy-start(f32[2,96,128]{2,0,1:T(2,128)} %copy-done.11) | copy-start | bytes 294916
  506.3 48.9 %copy-start.18 = (f32[2,96,128]{2,0,1:T(2,128)S(1)}, f32[2,96,128]{2,0,1:T(2,128)}, u32[]{:S(2)}) copy-start(f32[2,96,128]{2,0,1:T(2,128)} %get-tuple-element.103) | copy-start | bytes 294916
  506.4 49.1 %copy-start.38 = (f32[2,96,128]{2,1,0:T(8,128)S(1)}, f32[2,96,128]{2,1,0:T(8,128)}, u32[]{:S(2)}) copy-start(f32[2,96,128]{2,1,0:T(8,128)} %param.25) | copy-start | bytes 294916
  506.4 49.1 %copy-start.39 = (f32[2,96,128]{2,0,1:T(2,128)S(1)}, f32[2,96,128]{2,0,1:T(2,128)}, u32[]{:S(2)}) copy-start(f32[2,96,128]{2,0,1:T(2,128)} %get-tuple-element.101) | copy-start | bytes 294916
  (45 other events, 498.6 us)
Sparse Core Ops, SparseCore 0:
  18.2 58.9 reduce-scatter.24
  85.5 59.7 reduce-scatter.26
  153.8 59.6 reduce-scatter.28
  221.8 59.7 reduce-scatter.30
  290.3 59.7 reduce-scatter.32
  358.3 59.6 reduce-scatter.34
  426.7 59.6 reduce-scatter.36
  494.5 59.6 reduce-scatter.38
where the time goes:
time: 568 us; the launch traced here: 563 us
  waiting for transfers between devices  328 us (58%)
  starting transfers between devices  88.5 us (16%)
  local copies, waits for them, and re-layouts  80.6 us (14%)
  other arithmetic  51.2 us (9%)
  between operations  14.8 us (3%)
    unnamed x16, waiting for transfers between devices  328 us
    ppermute x16, starting transfers between devices, extended(): after = lax.ppermute(first, axis, down)  68.1 us
    unnamed x147, local copies, waits for them, and re-layouts  46.9 us
    ppermute x16, starting transfers between devices, extended(): before = lax.ppermute(last, axis, up)  20.1 us
    scatter-add x8, other arithmetic, fold_term(): placed = jnp.zeros((top_row.shape[0], columns * lax.axis_size('lon')), to...  15.5 us
    concatenate x16, other arithmetic, extended(): value = jnp.concatenate([before, value, after], axis=dim)  13.3 us
    concatenate x8, local copies, waits for them, and re-layouts, extended(): value = jnp.concatenate([before, value, after], axis=dim)  13.2 us
    add x8, other arithmetic, spread_field(): total + wide[index_dir, :, 1 - shift_lat:1 - shift_lat + rows, 1 - shift_...  13 us
  transfers between devices with their start and end apart: 40, of which 8 were waited for; matrix products, arithmetic and copies ran while one was open for 20% of the time, Pallas kernels for 0%

commit v1 on v0

v1 whole, which is shorter than its diff:
```python
import functools

import jax
import jax.numpy as jnp
from jax import lax
from jax.experimental import pallas as pl
from jax.experimental.pallas import tpu as pltpu
from jax.sharding import PartitionSpec as P

STEPS = 2
ITERS = 4
DEPTH = STEPS * ITERS
LANES = 128

OFFSETS = ((1, 0), (-1, 0), (0, 1), (0, -1), (1, 1), (1, -1), (-1, 1), (-1, -1))
TURNED = tuple(OFFSETS.index((-r, -c)) for r, c in OFFSETS)
CENTRE_VALUE = 1.05
HALF_WIDTH = 0.9
MESH = pl.DeviceIdType.MESH


def flipped(tile):
    lanes = lax.broadcasted_iota(jnp.int32, tile.shape, 1)
    rows = lax.broadcasted_iota(jnp.int32, tile.shape, 0)
    tile = jnp.take_along_axis(tile, tile.shape[1] - 1 - lanes, axis=1)
    for bit in (4, 2, 1):
        up = pltpu.roll(tile, bit, 0)
        down = pltpu.roll(tile, tile.shape[0] - bit, 0)
        tile = jnp.where((rows & bit) != 0, up, down)
    return tile


def kernel(
    n_lon,
    forcing,
    coeffs,
    sea_mask,
    fold,
    norm,
    out,
    to_partner,
    to_mirror,
    north,
    south,
    ext,
    weights,
    send_sems,
    recv_sems,
):
    levels, rows, cols = forcing.shape
    fields = 10 * levels
    pm_at = 8 * levels
    z_at = 9 * levels
    lon = lax.axis_index("lon")
    lat = lax.axis_index("lat")
    east = lax.rem(lon + 1, n_lon)
    west = lax.rem(lon + n_lon - 1, n_lon)
    mirror = n_lon - 1 - lon
    is_top = lat == 1

    barrier = pltpu.get_barrier_semaphore()

    def greet(where):
        pl.semaphore_signal(barrier, inc=1, device_id=where, device_id_type=MESH)

    greet({"lon": east})
    greet({"lon": west})
    greet({"lat": 1 - lat})

    @pl.when(is_top)
    def _():
        greet({"lon": mirror})

    lane = lax.broadcasted_iota(jnp.int32, (1, cols), 1)
    offset = fold[pl.ds(lon, 1), :] - (n_lon * cols - 1 - (lon * cols + lane))
    offset = jnp.where(offset < 0, offset + n_lon * cols, offset)
    row = lax.broadcasted_iota(jnp.int32, (8, cols), 0)
    at_fold = jnp.logical_and(row == 7, is_top)
    padding = jnp.zeros((LANES - rows, cols), jnp.float32)

    def keep(index, value):
        to_partner[index] = jnp.where(is_top, value[:8], value[rows - 8 :])
        level = index % levels
        group = index // levels
        turned = TURNED[group] if group < 8 else group
        to_mirror[turned * levels + level] = flipped(value[rows - 8 :])
        whole = jnp.concatenate([value, padding], axis=0)
        ext[index, DEPTH : DEPTH + cols, :] = whole.T

    for k in range(levels):
        diag_sum = coeffs[0, k]
        for d in range(1, 8):
            diag_sum = diag_sum + coeffs[d, k]
        sea = sea_mask[k].astype(jnp.float32)
        keep(pm_at + k, sea * (1.0 / (1.0 + diag_sum)))
        keep(z_at + k, sea * norm[k] * forcing[k])
        north_edge = coeffs[0, k, rows - 8 :, :]
        for d, (shift_lat, shift_lon) in enumerate(OFFSETS):
            value = coeffs[d, k]
            if shift_lat == 1:
                split = jnp.where(offset == 1 - shift_lon, north_edge, 0.0)
                edge = jnp.where(at_fold, split, value[rows - 8 :])
                value = jnp.concatenate([value[: rows - 8], edge], axis=0)
            keep(d * levels + k, value)

    def remote(source, target, which, where):
        return pltpu.make_async_remote_copy(
            src_ref=source,
            dst_ref=target,
            send_sem=send_sems.at[which],
            recv_sem=recv_sems.at[which],
            device_id=where,
            device_id_type=MESH,
        )

    down = remote(to_partner, north, 0, {"lat": 1 - lat})
    across = remote(to_mirror, north, 1, {"lon": mirror})
    up = remote(to_partner, south, 2, {"lat": 1 - lat})

    @pl.when(is_top)
    def _():
        pl.semaphore_wait(barrier, 4)
        across.start()
        down.start()

    @pl.when(jnp.logical_not(is_top))
    def _():
        pl.semaphore_wait(barrier, 3)
        up.start()
        south[...] = jnp.zeros_like(south)

    @pl.when(is_top)
    def _():
        up.wait_recv()
        across.wait_recv()

    @pl.when(jnp.logical_not(is_top))
    def _():
        down.wait_recv()

    nothing = jnp.zeros((8, cols), jnp.float32)
    for index in range(fields):
        plain = north[index]
        halo = jnp.concatenate(
            [
                jnp.where(is_top, pltpu.roll(plain, 1, 1), plain),
                jnp.where(is_top, plain, 0.0),
                nothing,
                south[index],
            ],
            axis=0,
        )
        ext[index, DEPTH : DEPTH + cols, rows : rows + 32] = halo.T

    total = cols + 2 * DEPTH
    go_west = remote(
        ext.at[:, pl.ds(DEPTH, DEPTH)], ext.at[:, pl.ds(DEPTH + cols, DEPTH)], 3, {"lon": west}
    )
    go_east = remote(ext.at[:, pl.ds(cols, DEPTH)], ext.at[:, pl.ds(0, DEPTH)], 4, {"lon": east})
    go_west.start()
    go_east.start()
    go_west.wait()
    go_east.wait()

    lane_row = lax.broadcasted_iota(jnp.int32, (fields, LANES), 1)
    ghost = jnp.logical_and(jnp.logical_and(lane_row >= rows, lane_row < rows + 8), is_top)
    for seam in (DEPTH, DEPTH + cols):
        before = pltpu.roll(ext[:, seam - 1, :], LANES - 8, 1)
        ext[:, seam, :] = jnp.where(ghost, before, ext[:, seam, :])

    lane_all = lax.broadcasted_iota(jnp.int32, (total, LANES), 1)
    inside = jnp.logical_or(lane_all < rows + 8, lane_all >= LANES - 8)

    def turn(value, shift, axis):
        shift = shift % value.shape[axis]
        return value if shift == 0 else pltpu.roll(value, shift, axis)

    scale = []
    for k in range(levels):
        pm = jnp.where(inside, ext[pm_at + k], 0.0)
        ext[pm_at + k] = pm
        pm_by = {c: turn(pm, -c, 0) for c in (-1, 0, 1)}
        for d, (shift_lat, shift_lon) in enumerate(OFFSETS):
            source = turn(ext[d * levels + k], shift_lat, 1)
            weights[d * levels + k] = pm_by[shift_lon] * source

    def spread(u, k):
        by_lat = {r: turn(u, r, 1) for r in (-1, 0, 1)}
        groups = {}
        for d, (shift_lat, shift_lon) in enumerate(OFFSETS):
            term = weights[d * levels + k] * by_lat[shift_lat]
            groups[shift_lon] = groups[shift_lon] + term if shift_lon in groups else term
        return groups[0] + turn(groups[1], 1, 0) + turn(groups[-1], -1, 0)

    sigma_ratio = CENTRE_VALUE / HALF_WIDTH
    state = [ext[z_at + k] for k in range(levels)]
    for step in range(STEPS):
        ratio_now = 1.0 / sigma_ratio
        scaled = [ext[pm_at + k] * state[k] for k in range(levels)]
        update = [value * (1.0 / CENTRE_VALUE) for value in scaled]
        state = list(update)
        for sweep in range(ITERS):
            ratio_next = 1.0 / (2.0 * sigma_ratio - ratio_now)
            for k in range(levels):
                scaled[k] = scaled[k] - update[k] + spread(update[k], k)
                update[k] = (ratio_next * ratio_now) * update[k] + (
                    2.0 * ratio_next / HALF_WIDTH
                ) * scaled[k]
                state[k] = state[k] + update[k]
            ratio_now = ratio_next

    for k in range(levels):
        own = state[k][DEPTH : DEPTH + cols].T
        out[k] = norm[k] * own[:rows]

    @pl.when(is_top)
    def _():
        down.wait_send()
        across.wait_send()

    @pl.when(jnp.logical_not(is_top))
    def _():
        up.wait_send()


def body(n_lon, forcing, coeffs, sea_mask, fold_pair, norm_scale):
    levels, rows, cols = forcing.shape
    fields = 10 * levels
    edge = pltpu.VMEM((fields, 8, cols), jnp.float32)
    return pl.pallas_call(
        functools.partial(kernel, n_lon),
        out_shape=jax.ShapeDtypeStruct(forcing.shape, jnp.float32),
        in_specs=[pl.BlockSpec(memory_space=pltpu.VMEM)] * 5,
        out_specs=pl.BlockSpec(memory_space=pltpu.VMEM),
        scratch_shapes=[
            edge,
            edge,
            edge,
            edge,
            pltpu.VMEM((fields, cols + 2 * DEPTH, LANES), jnp.float32),
            pltpu.VMEM((8 * levels, cols + 2 * DEPTH, LANES), jnp.float32),
            pltpu.SemaphoreType.DMA((5,)),
            pltpu.SemaphoreType.DMA((5,)),
        ],
        compiler_params=pltpu.CompilerParams(
            collective_id=0, has_side_effects=True, vmem_limit_bytes=32 * 1024 * 1024
        ),
    )(forcing, coeffs, sea_mask, fold_pair.reshape(n_lon, cols), norm_scale)


def solution(mesh):
    placed = (
        P("member", "lat", "lon"),
        P(None, None, "lat", "lon"),
        P(None, "lat", "lon"),
        P(),
        P(None, "lat", "lon"),
    )
    return jax.shard_map(
        functools.partial(body, mesh.shape["lon"]),
        mesh=mesh,
        in_specs=placed,
        out_specs=P("member", "lat", "lon"),
        check_vma=False,
    )
```

time: 568 us -> 23.1 us (0.04)
  waiting for transfers between devices: 328 us -> 0 us
  starting transfers between devices: 88.5 us -> 0 us
  local copies, waits for them, and re-layouts: 80.6 us -> 5.14 us
  other arithmetic: 51.2 us -> 0 us
  Pallas kernels: 0 us -> 17.7 us
  between operations: 14.8 us -> 0.01 us
    unnamed x16 -> x0, waiting for transfers between devices: 328 us -> none
    ppermute x32 -> x0, starting transfers between devices: 88.2 us -> none  [the longest x16 68.1 us: extended(): after = lax.ppermute(first, axis, down)]
    unnamed x147 -> x11, local copies, waits for them, and re-layouts: 46.9 us -> 5.14 us
    pallas_call x0 -> x1, Pallas kernels: none -> 17.7 us  [body(): pl.pallas_call(functools.partial(kernel, n_lon), out_shape=jax.ShapeDtype...]
    add x16 -> x0, other arithmetic: 17.5 us -> none  [the longest x8 13 us: spread_field(): total + wide[index_dir, :, 1 - shift_lat:1 - shift_lat + rows, 1 - shift_...]
    scatter-add x16 -> x0, other arithmetic: 15.6 us -> none  [the longest x8 15.5 us: fold_term(): placed = jnp.zeros((top_row.shape[0], columns * lax.axis_size('lon')), to...]
    concatenate x16 -> x0, other arithmetic: 13.3 us -> none  [extended(): value = jnp.concatenate([before, value, after], axis=dim)]
    concatenate x8 -> x0, local copies, waits for them, and re-layouts: 13.2 us -> none  [extended(): value = jnp.concatenate([before, value, after], axis=dim)]
  transfers between devices with their start and end apart: 40 -> 0, of which waited for: 8 -> 0; matrix products, arithmetic and copies ran while one was open for 20% -> 0% of each run, Pallas kernels for 0% -> 0%
where the time goes in v1:
time: 23.1 us; the launch traced here: 22.8 us
  Pallas kernels  17.7 us (77%)
  local copies, waits for them, and re-layouts  5.14 us (22%)
    pallas_call x1, Pallas kernels, body(): pl.pallas_call(functools.partial(kernel, n_lon), out_shape=jax.ShapeDtype...  17.7 us
    unnamed x11, local copies, waits for them, and re-layouts  5.14 us

profile of v1, /device:TPU:1, one launch (start us, length us, event | category | flops | bytes accessed | tf_op | source)
XLA Modules:
  0.0 22.8 jit_solution(2123876673907532352)
XLA Ops:
  0.0 0.0 copy-start
  0.0 1.1 %copy-done = f32[8,2,96,128]{3,2,1,0:T(8,128)S(1)} copy-done((f32[8,2,96,128]{3,2,1,0:T(8,128)S(1)}, f32[8,2,96,128]{3,2,1,0:T(8,128)}, u32[]{:S(2)}) %copy-start) | copy-done | bytes 786456
  1.1 0.0 copy-start.1
  1.1 0.9 %copy-done.1 = f32[2,96,128]{2,1,0:T(8,128)S(1)} copy-done((f32[2,96,128]{2,1,0:T(8,128)S(1)}, f32[2,96,128]{2,1,0:T(8,128)}, u32[]{:S(2)}) %copy-start.1) | copy-done | bytes 98328
  2.0 0.0 copy-start.2
  2.0 0.9 %copy-done.2 = s32[2,96,128]{2,1,0:T(8,128)S(1)} copy-done((s32[2,96,128]{2,1,0:T(8,128)S(1)}, s32[2,96,128]{2,1,0:T(8,128)}, u32[]{:S(2)}) %copy-start.2) | copy-done | bytes 98328
  2.9 0.0 copy-start.3
  2.9 0.9 %copy-done.3 = f32[2,96,128]{2,1,0:T(8,128)S(1)} copy-done((f32[2,96,128]{2,1,0:T(8,128)S(1)}, f32[2,96,128]{2,1,0:T(8,128)}, u32[]{:S(2)}) %copy-start.3) | copy-done | bytes 98328
  3.8 0.0 copy-start.4
  3.8 0.7 %copy-done.4 = s32[1024]{0:T(1024)S(1)} copy-done((s32[1024]{0:T(1024)S(1)}, s32[1024]{0:T(1024)}, u32[]{:S(2)}) %copy-start.4) | copy-done | bytes 4120
  4.5 17.7 %shard_map.55 = f32[2,96,128]{2,1,0:T(8,128)S(1)} custom-call(f32[2,96,128]{2,1,0:T(8,128)S(1)} %copy-done.1, f32[8,2,96,128]{3,2,1,0:T(8,128)S(1)} %copy-done, s32[2,96,128]{2,1,0:T(8,128)S(1)} %copy-done.2, s32[8,128]{1,0:T(8,128)S(1)} %bitcast.1, f32[2,96,128]{2,1,0:T(8,128)S(1)} %copy-done.3), custom_call_target="tpu_custom_call" | custom-call | tf_op jit(solution)/shard_map/pallas_call | solution.py:230
  22.2 0.6 %copy.7 = f32[2,96,128]{2,1,0:T(8,128)} copy(f32[2,96,128]{2,1,0:T(8,128)S(1)} %shard_map.55) | data formatting | bytes 196608
Async XLA Ops:
  0.0 1.1 %copy-start = (f32[8,2,96,128]{3,2,1,0:T(8,128)S(1)}, f32[8,2,96,128]{3,2,1,0:T(8,128)}, u32[]{:S(2)}) copy-start(f32[8,2,96,128]{3,2,1,0:T(8,128)} %coeffs.1) | copy-start | bytes 2359300
  1.1 0.9 %copy-start.1 = (f32[2,96,128]{2,1,0:T(8,128)S(1)}, f32[2,96,128]{2,1,0:T(8,128)}, u32[]{:S(2)}) copy-start(f32[2,96,128]{2,1,0:T(8,128)} %forcing.1) | copy-start | bytes 294916
  2.0 0.9 %copy-start.2 = (s32[2,96,128]{2,1,0:T(8,128)S(1)}, s32[2,96,128]{2,1,0:T(8,128)}, u32[]{:S(2)}) copy-start(s32[2,96,128]{2,1,0:T(8,128)} %sea_mask.1) | copy-start | bytes 294916
  2.9 0.9 %copy-start.3 = (f32[2,96,128]{2,1,0:T(8,128)S(1)}, f32[2,96,128]{2,1,0:T(8,128)}, u32[]{:S(2)}) copy-start(f32[2,96,128]{2,1,0:T(8,128)} %norm.1) | copy-start | bytes 294916
  3.8 0.7 %copy-start.4 = (s32[1024]{0:T(1024)S(1)}, s32[1024]{0:T(1024)}, u32[]{:S(2)}) copy-start(s32[1024]{0:T(1024)} %param.8) | copy-start | bytes 12292

commit v2 on v1

v2 whole, which is shorter than its diff:
```python
import functools

import jax
import jax.numpy as jnp
from jax import lax
from jax.experimental import pallas as pl
from jax.experimental.pallas import tpu as pltpu
from jax.sharding import PartitionSpec as P

STEPS = 2
ITERS = 4
DEPTH = STEPS * ITERS
LANES = 128

OFFSETS = ((1, 0), (-1, 0), (0, 1), (0, -1), (1, 1), (1, -1), (-1, 1), (-1, -1))
TURNED = tuple(OFFSETS.index((-r, -c)) for r, c in OFFSETS)
CENTRE_VALUE = 1.05
HALF_WIDTH = 0.9
MESH = pl.DeviceIdType.MESH


def flipped(tile):
    lanes = lax.broadcasted_iota(jnp.int32, tile.shape, 1)
    rows = lax.broadcasted_iota(jnp.int32, tile.shape, 0)
    tile = jnp.take_along_axis(tile, tile.shape[1] - 1 - lanes, axis=1)
    for bit in (4, 2, 1):
        up = pltpu.roll(tile, bit, 0)
        down = pltpu.roll(tile, tile.shape[0] - bit, 0)
        tile = jnp.where((rows & bit) != 0, up, down)
    return tile


def kernel(
    n_lon,
    forcing_hbm,
    coeffs_hbm,
    mask_hbm,
    fold_hbm,
    norm_hbm,
    out,
    forcing,
    coeffs,
    sea_mask,
    fold,
    norm,
    to_partner,
    to_mirror,
    north,
    south,
    ext,
    weights,
    update,
    residual,
    iterate,
    load_sems,
    send_sems,
    recv_sems,
):
    levels, rows, cols = forcing.shape
    fields = 10 * levels
    pm_at = 8 * levels
    z_at = 9 * levels
    total = cols + 2 * DEPTH
    lon = lax.axis_index("lon")
    lat = lax.axis_index("lat")
    east = lax.rem(lon + 1, n_lon)
    west = lax.rem(lon + n_lon - 1, n_lon)
    mirror = n_lon - 1 - lon
    is_top = lat == 1

    loads = [
        pltpu.make_async_copy(source, target, load_sems.at[i])
        for i, (source, target) in enumerate(
            (
                (coeffs_hbm, coeffs),
                (forcing_hbm, forcing),
                (mask_hbm, sea_mask),
                (norm_hbm, norm),
                (fold_hbm, fold),
            )
        )
    ]
    for load in loads:
        load.start()

    barrier = pltpu.get_barrier_semaphore()

    def greet(where):
        pl.semaphore_signal(barrier, inc=1, device_id=where, device_id_type=MESH)

    greet({"lon": east})
    greet({"lon": west})
    greet({"lat": 1 - lat})

    @pl.when(is_top)
    def _():
        greet({"lon": mirror})

    for load in loads:
        load.wait()

    lane = lax.broadcasted_iota(jnp.int32, (1, cols), 1)
    offset = fold[pl.ds(lon, 1), :] - (n_lon * cols - 1 - (lon * cols + lane))
    offset = jnp.where(offset < 0, offset + n_lon * cols, offset)
    sub = lax.broadcasted_iota(jnp.int32, (8, cols), 0)
    at_fold = jnp.logical_and(sub == 7, is_top)

    def fields_of(k, start, stop):
        c = [coeffs[d, k, start:stop, :] for d in range(8)]
        diag_sum = c[0]
        for d in range(1, 8):
            diag_sum = diag_sum + c[d]
        sea = sea_mask[k, start:stop, :].astype(jnp.float32)
        pm = sea * (1.0 / (1.0 + diag_sum))
        if stop == rows:
            cut = rows - 8 - start
            north_edge = c[0][cut:]
            for d, (shift_lat, shift_lon) in enumerate(OFFSETS):
                if shift_lat == 1:
                    split = jnp.where(offset == 1 - shift_lon, north_edge, 0.0)
                    edge = jnp.where(at_fold, split, c[d][cut:])
                    c[d] = jnp.concatenate([c[d][:cut], edge], axis=0) if cut else edge
        z = sea * norm[k, start:stop, :] * forcing[k, start:stop, :]
        return [value * pm for value in c] + [pm, z]

    for k in range(levels):
        top = fields_of(k, rows - 8, rows)
        bottom = fields_of(k, 0, 8)
        for group in range(10):
            to_partner[group * levels + k] = jnp.where(is_top, bottom[group], top[group])
            turned = TURNED[group] if group < 8 else group
            to_mirror[turned * levels + k] = flipped(top[group])

    def remote(source, target, which, where):
        return pltpu.make_async_remote_copy(
            src_ref=source,
            dst_ref=target,
            send_sem=send_sems.at[which],
            recv_sem=recv_sems.at[which],
            device_id=where,
            device_id_type=MESH,
        )

    down = remote(to_partner, north, 0, {"lat": 1 - lat})
    across = remote(to_mirror, north, 1, {"lon": mirror})
    up = remote(to_partner, south, 2, {"lat": 1 - lat})

    @pl.when(is_top)
    def _():
        pl.semaphore_wait(barrier, 4)
        across.start()
        down.start()

    @pl.when(jnp.logical_not(is_top))
    def _():
        pl.semaphore_wait(barrier, 3)
        up.start()
        south[...] = jnp.zeros_like(south)

    padding = jnp.zeros((LANES - rows, cols), jnp.float32)
    for k in range(levels):
        for group, value in enumerate(fields_of(k, 0, rows)):
            whole = jnp.concatenate([value, padding], axis=0)
            ext[group * levels + k, DEPTH : DEPTH + cols, :] = whole.T

    @pl.when(is_top)
    def _():
        up.wait_recv()
        across.wait_recv()

    @pl.when(jnp.logical_not(is_top))
    def _():
        down.wait_recv()

    nothing = jnp.zeros((8, cols), jnp.float32)
    for first in range(0, fields, 4):
        several = range(first, min(first + 4, fields))
        halo = []
        for index in several:
            plain = north[index]
            halo += [
                jnp.where(is_top, pltpu.roll(plain, 1, 1), plain),
                jnp.where(is_top, plain, 0.0),
                nothing,
                south[index],
            ]
        halo = jnp.concatenate(halo, axis=0).T
        for i, index in enumerate(several):
            ext[index, DEPTH : DEPTH + cols, LANES - 32 :] = halo[:, 32 * i : 32 * i + 32]

    go_west = remote(
        ext.at[:, pl.ds(DEPTH, DEPTH)], ext.at[:, pl.ds(DEPTH + cols, DEPTH)], 3, {"lon": west}
    )
    go_east = remote(ext.at[:, pl.ds(cols, DEPTH)], ext.at[:, pl.ds(0, DEPTH)], 4, {"lon": east})
    go_west.start()
    go_east.start()

    def place(start, stop):
        lanes = lax.broadcasted_iota(jnp.int32, (stop - start, LANES), 1)
        inside = jnp.logical_or(lanes < rows + 8, lanes >= LANES - 8)
        for k in range(levels):
            for d, (shift_lat, _) in enumerate(OFFSETS):
                value = jnp.where(inside, ext[d * levels + k, start:stop, :], 0.0)
                if shift_lat:
                    value = pltpu.roll(value, shift_lat % LANES, 1)
                weights[d * levels + k, start:stop, :] = value

    place(2 * DEPTH, DEPTH + cols)
    go_west.wait()
    go_east.wait()

    lane_row = lax.broadcasted_iota(jnp.int32, (fields, LANES), 1)
    ghost = jnp.logical_and(jnp.logical_and(lane_row >= rows, lane_row < rows + 8), is_top)
    for seam in (DEPTH, DEPTH + cols):
        before = pltpu.roll(ext[:, seam - 1, :], LANES - 8, 1)
        ext[:, seam, :] = jnp.where(ghost, before, ext[:, seam, :])
    place(0, 2 * DEPTH)
    place(DEPTH + cols, total)

    chunks = total // 8
    sub_all = lax.broadcasted_iota(jnp.int32, (8, LANES), 0)
    low, high = sub_all == 0, sub_all == 7

    def parts(k, s):
        at = pl.ds(8 * s, 8)
        u = update[k, at, :]
        by_lat = {0: u, 1: pltpu.roll(u, 1, 1), -1: pltpu.roll(u, LANES - 1, 1)}
        sums = {}
        for d, (shift_lat, shift_lon) in enumerate(OFFSETS):
            term = weights[d * levels + k, at, :] * by_lat[shift_lat]
            sums[shift_lon] = sums[shift_lon] + term if shift_lon in sums else term
        return sums[-1], sums[0], sums[1], u

    def sweep(keep_ratio, gain):
        held = [[None] * chunks for _ in range(levels)]
        for s in range(chunks + 1):
            for k in range(levels):
                if s < chunks:
                    held[k][s] = parts(k, s)
                if s == 0:
                    continue
                t = s - 1
                here = held[k][t]
                left = held[k][t - 1][2] if t else here[2]
                right = held[k][s][0] if s < chunks else here[0]
                gained = (
                    here[1]
                    + pltpu.roll(jnp.where(high, left, here[2]), 1, 0)
                    + pltpu.roll(jnp.where(low, right, here[0]), 7, 0)
                )
                at = pl.ds(8 * t, 8)
                res = (residual[k, at, :] - here[3]) + gained
                new = keep_ratio * here[3] + gain * res
                residual[k, at, :] = res
                update[k, at, :] = new
                iterate[k, at, :] = iterate[k, at, :] + new

    sigma_ratio = CENTRE_VALUE / HALF_WIDTH
    ratio_now = 1.0 / sigma_ratio
    factors = []
    for _ in range(ITERS):
        ratio_next = 1.0 / (2.0 * sigma_ratio - ratio_now)
        factors.append((ratio_next * ratio_now, 2.0 * ratio_next / HALF_WIDTH))
        ratio_now = ratio_next

    def pick(values, i):
        chosen = jnp.float32(values[-1])
        for n in range(len(values) - 1):
            chosen = jnp.where(i == n, jnp.float32(values[n]), chosen)
        return chosen

    for step in range(STEPS):
        for k in range(levels):
            start = ext[z_at + k] if step == 0 else ext[pm_at + k] * iterate[k]
            residual[k] = start
            first = start * (1.0 / CENTRE_VALUE)
            update[k] = first
            iterate[k] = first

        @pl.loop(0, ITERS)
        def _(i):
            sweep(pick([f[0] for f in factors], i), pick([f[1] for f in factors], i))

    for k in range(levels):
        own = (ext[pm_at + k, DEPTH : DEPTH + cols] * iterate[k, DEPTH : DEPTH + cols]).T
        out[k] = norm[k] * own[:rows]

    @pl.when(is_top)
    def _():
        down.wait_send()
        across.wait_send()

    @pl.when(jnp.logical_not(is_top))
    def _():
        up.wait_send()


def body(n_lon, forcing, coeffs, sea_mask, fold_pair, norm_scale):
    levels, rows, cols = forcing.shape
    fields = 10 * levels
    total = cols + 2 * DEPTH
    edge = pltpu.VMEM((fields, 8, cols), jnp.float32)
    tile = pltpu.VMEM(forcing.shape, jnp.float32)
    field = pltpu.VMEM((levels, total, LANES), jnp.float32)
    return pl.pallas_call(
        functools.partial(kernel, n_lon),
        out_shape=jax.ShapeDtypeStruct(forcing.shape, jnp.float32),
        in_specs=[pl.BlockSpec(memory_space=pltpu.HBM)] * 5,
        out_specs=pl.BlockSpec(memory_space=pltpu.VMEM),
        scratch_shapes=[
            tile,
            pltpu.VMEM(coeffs.shape, jnp.float32),
            pltpu.VMEM(sea_mask.shape, jnp.int32),
            pltpu.VMEM((n_lon, cols), jnp.int32),
            tile,
            edge,
            edge,
            edge,
            edge,
            pltpu.VMEM((fields, total, LANES), jnp.float32),
            pltpu.VMEM((8 * levels, total, LANES), jnp.float32),
            field,
            field,
            field,
            pltpu.SemaphoreType.DMA((5,)),
            pltpu.SemaphoreType.DMA((5,)),
            pltpu.SemaphoreType.DMA((5,)),
        ],
        compiler_params=pltpu.CompilerParams(
            collective_id=0, has_side_effects=True, vmem_limit_bytes=32 * 1024 * 1024
        ),
    )(forcing, coeffs, sea_mask, fold_pair.reshape(n_lon, cols), norm_scale)


def solution(mesh):
    placed = (
        P("member", "lat", "lon"),
        P(None, None, "lat", "lon"),
        P(None, "lat", "lon"),
        P(),
        P(None, "lat", "lon"),
    )
    return jax.shard_map(
        functools.partial(body, mesh.shape["lon"]),
        mesh=mesh,
        in_specs=placed,
        out_specs=P("member", "lat", "lon"),
        check_vma=False,
    )
```

time: 23.1 us -> 22 us (0.952)
  Pallas kernels: 17.7 us -> 16.6 us
    pallas_call x1, Pallas kernels: 17.7 us -> 16.6 us  [body(): pl.pallas_call(functools.partial(kernel, n_lon), out_shape=jax.ShapeDtype...]
where the time goes in v2:
time: 22 us; the launch traced here: 21.7 us
  Pallas kernels  16.6 us (75%)
  local copies, waits for them, and re-layouts  5.14 us (23%)
    pallas_call x1, Pallas kernels, body(): pl.pallas_call(functools.partial(kernel, n_lon), out_shape=jax.ShapeDtype...  16.6 us
    unnamed x11, local copies, waits for them, and re-layouts  5.14 us

profile of v2, /device:TPU:1, one launch (start us, length us, event | category | flops | bytes accessed | tf_op | source)
XLA Modules:
  0.0 21.7 jit_solution(1052818819719937948)
XLA Ops:
  0.0 0.0 copy-start
  0.0 1.1 %copy-done = f32[8,2,96,128]{3,2,1,0:T(8,128)S(1)} copy-done((f32[8,2,96,128]{3,2,1,0:T(8,128)S(1)}, f32[8,2,96,128]{3,2,1,0:T(8,128)}, u32[]{:S(2)}) %copy-start) | copy-done | bytes 786456
  1.1 0.0 copy-start.1
  1.1 0.9 %copy-done.1 = f32[2,96,128]{2,1,0:T(8,128)S(1)} copy-done((f32[2,96,128]{2,1,0:T(8,128)S(1)}, f32[2,96,128]{2,1,0:T(8,128)}, u32[]{:S(2)}) %copy-start.1) | copy-done | bytes 98328
  2.0 0.0 copy-start.2
  2.0 0.9 %copy-done.2 = s32[2,96,128]{2,1,0:T(8,128)S(1)} copy-done((s32[2,96,128]{2,1,0:T(8,128)S(1)}, s32[2,96,128]{2,1,0:T(8,128)}, u32[]{:S(2)}) %copy-start.2) | copy-done | bytes 98328
  2.9 0.0 copy-start.3
  2.9 0.9 %copy-done.3 = f32[2,96,128]{2,1,0:T(8,128)S(1)} copy-done((f32[2,96,128]{2,1,0:T(8,128)S(1)}, f32[2,96,128]{2,1,0:T(8,128)}, u32[]{:S(2)}) %copy-start.3) | copy-done | bytes 98328
  3.8 0.0 copy-start.4
  3.8 0.7 %copy-done.4 = s32[1024]{0:T(1024)S(1)} copy-done((s32[1024]{0:T(1024)S(1)}, s32[1024]{0:T(1024)}, u32[]{:S(2)}) %copy-start.4) | copy-done | bytes 4120
  4.5 16.6 %shard_map.55 = f32[2,96,128]{2,1,0:T(8,128)S(1)} custom-call(f32[2,96,128]{2,1,0:T(8,128)S(1)} %copy-done.1, f32[8,2,96,128]{3,2,1,0:T(8,128)S(1)} %copy-done, s32[2,96,128]{2,1,0:T(8,128)S(1)} %copy-done.2, s32[8,128]{1,0:T(8,128)S(1)} %bitcast.1, f32[2,96,128]{2,1,0:T(8,128)S(1)} %copy-done.3), custom_call_target="tpu_custom_call" | custom-call | tf_op jit(solution)/shard_map/pallas_call | solution.py:305
  21.1 0.6 %copy.7 = f32[2,96,128]{2,1,0:T(8,128)} copy(f32[2,96,128]{2,1,0:T(8,128)S(1)} %shard_map.55) | data formatting | bytes 196608
Async XLA Ops:
  0.0 1.1 %copy-start = (f32[8,2,96,128]{3,2,1,0:T(8,128)S(1)}, f32[8,2,96,128]{3,2,1,0:T(8,128)}, u32[]{:S(2)}) copy-start(f32[8,2,96,128]{3,2,1,0:T(8,128)} %coeffs_hbm.1) | copy-start | bytes 2359300
  1.1 0.9 %copy-start.1 = (f32[2,96,128]{2,1,0:T(8,128)S(1)}, f32[2,96,128]{2,1,0:T(8,128)}, u32[]{:S(2)}) copy-start(f32[2,96,128]{2,1,0:T(8,128)} %forcing_hbm.1) | copy-start | bytes 294916
  2.0 0.9 %copy-start.2 = (s32[2,96,128]{2,1,0:T(8,128)S(1)}, s32[2,96,128]{2,1,0:T(8,128)}, u32[]{:S(2)}) copy-start(s32[2,96,128]{2,1,0:T(8,128)} %mask_hbm.1) | copy-start | bytes 294916
  2.9 0.9 %copy-start.3 = (f32[2,96,128]{2,1,0:T(8,128)S(1)}, f32[2,96,128]{2,1,0:T(8,128)}, u32[]{:S(2)}) copy-start(f32[2,96,128]{2,1,0:T(8,128)} %norm_hbm.1) | copy-start | bytes 294916
  3.8 0.7 %copy-start.4 = (s32[1024]{0:T(1024)S(1)}, s32[1024]{0:T(1024)}, u32[]{:S(2)}) copy-start(s32[1024]{0:T(1024)} %param.8) | copy-start | bytes 12292

commit v3 on v2

--- a/solution.py
+++ b/solution.py
@@ -327,7 +327,7 @@
             pltpu.SemaphoreType.DMA((5,)),
         ],
         compiler_params=pltpu.CompilerParams(
-            collective_id=0, has_side_effects=True, vmem_limit_bytes=32 * 1024 * 1024
+            collective_id=0, has_side_effects=True, vmem_limit_bytes=60 * 1024 * 1024
         ),
     )(forcing, coeffs, sea_mask, fold_pair.reshape(n_lon, cols), norm_scale)
 

time: 22 us -> 18.5 us (0.84)
  local copies, waits for them, and re-layouts: 5.14 us -> 1.54 us
    unnamed x11 -> x1, local copies, waits for them, and re-layouts: 5.14 us -> 1.54 us
where the time goes in v3:
time: 18.5 us; the launch traced here: 18.3 us
  Pallas kernels  16.7 us (90%)
  local copies, waits for them, and re-layouts  1.54 us (8%)
    pallas_call x1, Pallas kernels, body(): pl.pallas_call(functools.partial(kernel, n_lon), out_shape=jax.ShapeDtype...  16.7 us
    unnamed x1, local copies, waits for them, and re-layouts  1.54 us

profile of v3, /device:TPU:1, one launch (start us, length us, event | category | flops | bytes accessed | tf_op | source)
XLA Modules:
  0.0 18.3 jit_solution(13882185838188620652)
XLA Ops:
  0.0 16.7 %shard_map.55 = f32[2,96,128]{2,1,0:T(8,128)} custom-call(f32[2,96,128]{2,1,0:T(8,128)} %forcing_hbm.1, f32[8,2,96,128]{3,2,1,0:T(8,128)} %coeffs_hbm.1, s32[2,96,128]{2,1,0:T(8,128)} %mask_hbm.1, s32[8,128]{1,0:T(8,128)} %bitcast.1, f32[2,96,128]{2,1,0:T(8,128)} %norm_hbm.1), custom_call_target="tpu_custom_call" | custom-call | tf_op jit(solution)/shard_map/pallas_call | solution.py:305
  16.8 1.5 %copy.7 = f32[2,96,128]{2,1,0:T(8,128)} copy(f32[2,96,128]{2,1,0:T(8,128)} %shard_map.55) | data formatting | bytes 196608

commit v4 on v3

--- a/solution.py
+++ b/solution.py
@@ -48,6 +48,7 @@
     north,
     south,
     ext,
+    rim,
     weights,
     update,
     residual,
@@ -163,6 +164,24 @@
             whole = jnp.concatenate([value, padding], axis=0)
             ext[group * levels + k, DEPTH : DEPTH + cols, :] = whole.T
 
+    ends = ((DEPTH, DEPTH + cols, west), (cols, 0, east))
+
+    def strips(fields_ref, first):
+        return [
+            remote(
+                fields_ref.at[:, pl.ds(source, DEPTH)],
+                fields_ref.at[:, pl.ds(target, DEPTH)],
+                first + i,
+                {"lon": where},
+            )
+            for i, (source, target, where) in enumerate(ends)
+        ]
+
+    strip_sends = strips(ext, 3)
+    rim_sends = strips(rim, 5)
+    for send in strip_sends:
+        send.start()
+
     @pl.when(is_top)
     def _():
         up.wait_recv()
@@ -174,9 +193,8 @@
 
     nothing = jnp.zeros((8, cols), jnp.float32)
     for first in range(0, fields, 4):
-        several = range(first, min(first + 4, fields))
         halo = []
-        for index in several:
+        for index in range(first, first + 4):
             plain = north[index]
             halo += [
                 jnp.where(is_top, pltpu.roll(plain, 1, 1), plain),
@@ -184,16 +202,18 @@
                 nothing,
                 south[index],
             ]
-        halo = jnp.concatenate(halo, axis=0).T
-        for i, index in enumerate(several):
-            ext[index, DEPTH : DEPTH + cols, LANES - 32 :] = halo[:, 32 * i : 32 * i + 32]
-
-    go_west = remote(
-        ext.at[:, pl.ds(DEPTH, DEPTH)], ext.at[:, pl.ds(DEPTH + cols, DEPTH)], 3, {"lon": west}
-    )
-    go_east = remote(ext.at[:, pl.ds(cols, DEPTH)], ext.at[:, pl.ds(0, DEPTH)], 4, {"lon": east})
-    go_west.start()
-    go_east.start()
+        rim[first // 4, DEPTH : DEPTH + cols, :] = jnp.concatenate(halo, axis=0).T
+    for send in rim_sends:
+        send.start()
+    for send in strip_sends:
+        send.wait()
+
+    def merge(start, stop):
+        for index in range(fields):
+            at = 32 * (index % 4)
+            ext[index, start:stop, LANES - 32 :] = rim[index // 4, start:stop, at : at + 32]
+
+    merge(DEPTH, DEPTH + cols)
 
     def place(start, stop):
         lanes = lax.broadcasted_iota(jnp.int32, (stop - start, LANES), 1)
@@ -206,8 +226,10 @@
                 weights[d * levels + k, start:stop, :] = value
 
     place(2 * DEPTH, DEPTH + cols)
-    go_west.wait()
-    go_east.wait()
+    for send in rim_sends:
+        send.wait()
+    merge(0, DEPTH)
+    merge(DEPTH + cols, total)
 
     lane_row = lax.broadcasted_iota(jnp.int32, (fields, LANES), 1)
     ghost = jnp.logical_and(jnp.logical_and(lane_row >= rows, lane_row < rows + 8), is_top)
@@ -318,13 +340,14 @@
             edge,
             edge,
             pltpu.VMEM((fields, total, LANES), jnp.float32),
+            pltpu.VMEM((fields // 4, total, LANES), jnp.float32),
             pltpu.VMEM((8 * levels, total, LANES), jnp.float32),
             field,
             field,
             field,
             pltpu.SemaphoreType.DMA((5,)),
-            pltpu.SemaphoreType.DMA((5,)),
-            pltpu.SemaphoreType.DMA((5,)),
+            pltpu.SemaphoreType.DMA((7,)),
+            pltpu.SemaphoreType.DMA((7,)),
         ],
         compiler_params=pltpu.CompilerParams(
             collective_id=0, has_side_effects=True, vmem_limit_bytes=60 * 1024 * 1024

time: 18.5 us -> 17 us (0.919)
  Pallas kernels: 16.7 us -> 15.3 us
    pallas_call x1, Pallas kernels: 16.7 us -> 15.3 us  [body(): pl.pallas_call(functools.partial(kernel, n_lon), out_shape=jax.ShapeDtype...]
where the time goes in v4:
time: 17 us; the launch traced here: 16.8 us
  Pallas kernels  15.3 us (90%)
  local copies, waits for them, and re-layouts  1.54 us (9%)
    pallas_call x1, Pallas kernels, body(): pl.pallas_call(functools.partial(kernel, n_lon), out_shape=jax.ShapeDtype...  15.3 us
    unnamed x1, local copies, waits for them, and re-layouts  1.54 us

profile of v4, /device:TPU:1, one launch (start us, length us, event | category | flops | bytes accessed | tf_op | source)
XLA Modules:
  0.0 16.8 jit_solution(18335239553466243101)
XLA Ops:
  0.0 15.3 %shard_map.55 = f32[2,96,128]{2,1,0:T(8,128)} custom-call(f32[2,96,128]{2,1,0:T(8,128)} %forcing_hbm.1, f32[8,2,96,128]{3,2,1,0:T(8,128)} %coeffs_hbm.1, s32[2,96,128]{2,1,0:T(8,128)} %mask_hbm.1, s32[8,128]{1,0:T(8,128)} %bitcast.1, f32[2,96,128]{2,1,0:T(8,128)} %norm_hbm.1), custom_call_target="tpu_custom_call" | custom-call | tf_op jit(solution)/shard_map/pallas_call | solution.py:327
  15.3 1.5 %copy.7 = f32[2,96,128]{2,1,0:T(8,128)} copy(f32[2,96,128]{2,1,0:T(8,128)} %shard_map.55) | data formatting | bytes 196608

commit v5 on v4

--- a/solution.py
+++ b/solution.py
@@ -146,18 +146,6 @@
     across = remote(to_mirror, north, 1, {"lon": mirror})
     up = remote(to_partner, south, 2, {"lat": 1 - lat})
 
-    @pl.when(is_top)
-    def _():
-        pl.semaphore_wait(barrier, 4)
-        across.start()
-        down.start()
-
-    @pl.when(jnp.logical_not(is_top))
-    def _():
-        pl.semaphore_wait(barrier, 3)
-        up.start()
-        south[...] = jnp.zeros_like(south)
-
     padding = jnp.zeros((LANES - rows, cols), jnp.float32)
     for k in range(levels):
         for group, value in enumerate(fields_of(k, 0, rows)):
@@ -166,19 +154,42 @@
 
     ends = ((DEPTH, DEPTH + cols, west), (cols, 0, east))
 
-    def strips(fields_ref, first):
+    def strips(fields_ref, count, first):
         return [
             remote(
-                fields_ref.at[:, pl.ds(source, DEPTH)],
-                fields_ref.at[:, pl.ds(target, DEPTH)],
+                fields_ref.at[pl.ds(0, count), pl.ds(source, DEPTH)],
+                fields_ref.at[pl.ds(0, count), pl.ds(target, DEPTH)],
                 first + i,
                 {"lon": where},
             )
             for i, (source, target, where) in enumerate(ends)
         ]
 
-    strip_sends = strips(ext, 3)
-    rim_sends = strips(rim, 5)
+    sent = fields * 3 // 4
+
+    def thirds():
+        for i in range(sent):
+            yield i, sent + i // 3, 32 * (i % 3)
+
+    for start in (DEPTH, cols):
+        for carrier, rider, at in thirds():
+            piece = ext[rider, start : start + DEPTH, at : at + 32]
+            ext[carrier, start : start + DEPTH, LANES - 32 :] = piece
+
+    @pl.when(is_top)
+    def _():
+        pl.semaphore_wait(barrier, 4)
+        across.start()
+        down.start()
+
+    @pl.when(jnp.logical_not(is_top))
+    def _():
+        pl.semaphore_wait(barrier, 3)
+        up.start()
+        south[...] = jnp.zeros_like(south)
+
+    strip_sends = strips(ext, sent, 3)
+    rim_sends = strips(rim, fields // 4, 5)
     for send in strip_sends:
         send.start()
 
@@ -213,6 +224,10 @@
             at = 32 * (index % 4)
             ext[index, start:stop, LANES - 32 :] = rim[index // 4, start:stop, at : at + 32]
 
+    for start in (0, DEPTH + cols):
+        for carrier, rider, at in thirds():
+            piece = ext[carrier, start : start + DEPTH, LANES - 32 :]
+            ext[rider, start : start + DEPTH, at : at + 32] = piece
     merge(DEPTH, DEPTH + cols)
 
     def place(start, stop):

time: 17 us -> 17 us (level)
  no operation moved by 1% of the time
where the time goes in v5:
time: 17 us; the launch traced here: 16.8 us
  Pallas kernels  15.3 us (90%)
  local copies, waits for them, and re-layouts  1.54 us (9%)
    pallas_call x1, Pallas kernels, body(): pl.pallas_call(functools.partial(kernel, n_lon), out_shape=jax.ShapeDtype...  15.3 us
    unnamed x1, local copies, waits for them, and re-layouts  1.54 us

profile of v5, /device:TPU:1, one launch (start us, length us, event | category | flops | bytes accessed | tf_op | source)
XLA Modules:
  0.0 16.8 jit_solution(15938991752255081823)
XLA Ops:
  0.0 15.3 %shard_map.55 = f32[2,96,128]{2,1,0:T(8,128)} custom-call(f32[2,96,128]{2,1,0:T(8,128)} %forcing_hbm.1, f32[8,2,96,128]{3,2,1,0:T(8,128)} %coeffs_hbm.1, s32[2,96,128]{2,1,0:T(8,128)} %mask_hbm.1, s32[8,128]{1,0:T(8,128)} %bitcast.1, f32[2,96,128]{2,1,0:T(8,128)} %norm_hbm.1), custom_call_target="tpu_custom_call" | custom-call | tf_op jit(solution)/shard_map/pallas_call | solution.py:342
  15.3 1.5 %copy.7 = f32[2,96,128]{2,1,0:T(8,128)} copy(f32[2,96,128]{2,1,0:T(8,128)} %shard_map.55) | data formatting | bytes 196608

commit v6 on v5

--- a/solution.py
+++ b/solution.py
@@ -142,9 +142,20 @@
             device_id_type=MESH,
         )
 
-    down = remote(to_partner, north, 0, {"lat": 1 - lat})
-    across = remote(to_mirror, north, 1, {"lon": mirror})
-    up = remote(to_partner, south, 2, {"lat": 1 - lat})
+    middle = 4 * ((fields // 4 + 1) // 2)
+    halves = ((0, middle), (middle, fields))
+
+    def in_halves(source, target, which, where):
+        return [
+            remote(
+                source.at[pl.ds(a, b - a)], target.at[pl.ds(a, b - a)], which + i, where
+            )
+            for i, (a, b) in enumerate(halves)
+        ]
+
+    down = in_halves(to_partner, north, 0, {"lat": 1 - lat})
+    across = in_halves(to_mirror, north, 2, {"lon": mirror})
+    up = in_halves(to_partner, south, 4, {"lat": 1 - lat})
 
     padding = jnp.zeros((LANES - rows, cols), jnp.float32)
     for k in range(levels):
@@ -154,11 +165,11 @@
 
     ends = ((DEPTH, DEPTH + cols, west), (cols, 0, east))
 
-    def strips(fields_ref, count, first):
+    def strips(fields_ref, begin, count, first):
         return [
             remote(
-                fields_ref.at[pl.ds(0, count), pl.ds(source, DEPTH)],
-                fields_ref.at[pl.ds(0, count), pl.ds(target, DEPTH)],
+                fields_ref.at[pl.ds(begin, count), pl.ds(source, DEPTH)],
+                fields_ref.at[pl.ds(begin, count), pl.ds(target, DEPTH)],
                 first + i,
                 {"lon": where},
             )
@@ -179,43 +190,49 @@
     @pl.when(is_top)
     def _():
         pl.semaphore_wait(barrier, 4)
-        across.start()
-        down.start()
+        for i in range(2):
+            across[i].start()
+            down[i].start()
 
     @pl.when(jnp.logical_not(is_top))
     def _():
         pl.semaphore_wait(barrier, 3)
-        up.start()
+        for i in range(2):
+            up[i].start()
         south[...] = jnp.zeros_like(south)
 
-    strip_sends = strips(ext, sent, 3)
-    rim_sends = strips(rim, fields // 4, 5)
+    strip_sends = strips(ext, 0, sent, 6)
+    rim_sends = [
+        strips(rim, a // 4, (b - a) // 4, 8 + 2 * i) for i, (a, b) in enumerate(halves)
+    ]
     for send in strip_sends:
         send.start()
 
-    @pl.when(is_top)
-    def _():
-        up.wait_recv()
-        across.wait_recv()
-
-    @pl.when(jnp.logical_not(is_top))
-    def _():
-        down.wait_recv()
-
     nothing = jnp.zeros((8, cols), jnp.float32)
-    for first in range(0, fields, 4):
-        halo = []
-        for index in range(first, first + 4):
-            plain = north[index]
-            halo += [
-                jnp.where(is_top, pltpu.roll(plain, 1, 1), plain),
-                jnp.where(is_top, plain, 0.0),
-                nothing,
-                south[index],
-            ]
-        rim[first // 4, DEPTH : DEPTH + cols, :] = jnp.concatenate(halo, axis=0).T
-    for send in rim_sends:
-        send.start()
+    for half in range(2):
+
+        @pl.when(is_top)
+        def _():
+            up[half].wait_recv()
+            across[half].wait_recv()
+
+        @pl.when(jnp.logical_not(is_top))
+        def _():
+            down[half].wait_recv()
+
+        for first in range(*halves[half], 4):
+            halo = []
+            for index in range(first, first + 4):
+                plain = north[index]
+                halo += [
+                    jnp.where(is_top, pltpu.roll(plain, 1, 1), plain),
+                    jnp.where(is_top, plain, 0.0),
+                    nothing,
+                    south[index],
+                ]
+            rim[first // 4, DEPTH : DEPTH + cols, :] = jnp.concatenate(halo, axis=0).T
+        for send in rim_sends[half]:
+            send.start()
     for send in strip_sends:
         send.wait()
 
@@ -241,7 +258,7 @@
                 weights[d * levels + k, start:stop, :] = value
 
     place(2 * DEPTH, DEPTH + cols)
-    for send in rim_sends:
+    for send in rim_sends[0] + rim_sends[1]:
         send.wait()
     merge(0, DEPTH)
     merge(DEPTH + cols, total)
@@ -324,12 +341,14 @@
 
     @pl.when(is_top)
     def _():
-        down.wait_send()
-        across.wait_send()
+        for i in range(2):
+            down[i].wait_send()
+            across[i].wait_send()
 
     @pl.when(jnp.logical_not(is_top))
     def _():
-        up.wait_send()
+        for i in range(2):
+            up[i].wait_send()
 
 
 def body(n_lon, forcing, coeffs, sea_mask, fold_pair, norm_scale):
@@ -361,8 +380,8 @@
             field,
             field,
             pltpu.SemaphoreType.DMA((5,)),
-            pltpu.SemaphoreType.DMA((7,)),
-            pltpu.SemaphoreType.DMA((7,)),
+            pltpu.SemaphoreType.DMA((12,)),
+            pltpu.SemaphoreType.DMA((12,)),
         ],
         compiler_params=pltpu.CompilerParams(
             collective_id=0, has_side_effects=True, vmem_limit_bytes=60 * 1024 * 1024

time: 17 us -> 16.9 us (level)
  no operation moved by 1% of the time
where the time goes in v6:
time: 16.9 us; the launch traced here: 16.7 us
  Pallas kernels  15.2 us (90%)
  local copies, waits for them, and re-layouts  1.54 us (9%)
    pallas_call x1, Pallas kernels, body(): pl.pallas_call(functools.partial(kernel, n_lon), out_shape=jax.ShapeDtype...  15.2 us
    unnamed x1, local copies, waits for them, and re-layouts  1.54 us

profile of v6, /device:TPU:1, one launch (start us, length us, event | category | flops | bytes accessed | tf_op | source)
XLA Modules:
  0.0 16.7 jit_solution(6011935627223658503)
XLA Ops:
  0.0 15.2 %shard_map.55 = f32[2,96,128]{2,1,0:T(8,128)} custom-call(f32[2,96,128]{2,1,0:T(8,128)} %forcing_hbm.1, f32[8,2,96,128]{3,2,1,0:T(8,128)} %coeffs_hbm.1, s32[2,96,128]{2,1,0:T(8,128)} %mask_hbm.1, s32[8,128]{1,0:T(8,128)} %bitcast.1, f32[2,96,128]{2,1,0:T(8,128)} %norm_hbm.1), custom_call_target="tpu_custom_call" | custom-call | tf_op jit(solution)/shard_map/pallas_call | solution.py:361
  15.2 1.5 %copy.7 = f32[2,96,128]{2,1,0:T(8,128)} copy(f32[2,96,128]{2,1,0:T(8,128)} %shard_map.55) | data formatting | bytes 196608

commit v7 on v6

--- a/solution.py
+++ b/solution.py
@@ -337,7 +337,7 @@
 
     for k in range(levels):
         own = (ext[pm_at + k, DEPTH : DEPTH + cols] * iterate[k, DEPTH : DEPTH + cols]).T
-        out[k] = norm[k] * own[:rows]
+        out[k] = own[:rows]
 
     @pl.when(is_top)
     def _():
@@ -386,7 +386,7 @@
         compiler_params=pltpu.CompilerParams(
             collective_id=0, has_side_effects=True, vmem_limit_bytes=60 * 1024 * 1024
         ),
-    )(forcing, coeffs, sea_mask, fold_pair.reshape(n_lon, cols), norm_scale)
+    )(forcing, coeffs, sea_mask, fold_pair.reshape(n_lon, cols), norm_scale) * norm_scale
 
 
 def solution(mesh):

time: 16.9 us -> 16.9 us (level)
  other arithmetic: 0 us -> 1.55 us
  local copies, waits for them, and re-layouts: 1.54 us -> 0.01 us
    mul x0 -> x1, other arithmetic: none -> 1.55 us  [body(): pl.pallas_call(functools.partial(kernel, n_lon), out_shape=jax.ShapeDtype...]
    unnamed x1 -> x2, local copies, waits for them, and re-layouts: 1.54 us -> 0.01 us
where the time goes in v7:
time: 16.9 us; the launch traced here: 16.8 us
  Pallas kernels  15.2 us (90%)
  other arithmetic  1.55 us (9%)
    pallas_call x1, Pallas kernels, body(): pl.pallas_call(functools.partial(kernel, n_lon), out_shape=jax.ShapeDtype...  15.2 us
    mul x1, other arithmetic, body(): pl.pallas_call(functools.partial(kernel, n_lon), out_shape=jax.ShapeDtype...  1.55 us

profile of v7, /device:TPU:1, one launch (start us, length us, event | category | flops | bytes accessed | tf_op | source)
XLA Modules:
  0.0 16.8 jit_solution(16850508419241333170)
XLA Ops:
  0.0 0.0 copy-start
  0.0 15.2 %shard_map.55 = f32[2,96,128]{2,1,0:T(8,128)} custom-call(f32[2,96,128]{2,1,0:T(8,128)} %forcing_hbm.1, f32[8,2,96,128]{3,2,1,0:T(8,128)} %coeffs_hbm.1, s32[2,96,128]{2,1,0:T(8,128)} %mask_hbm.1, s32[8,128]{1,0:T(8,128)} %bitcast.1, f32[2,96,128]{2,1,0:T(8,128)} %norm_hbm.1), custom_call_target="tpu_custom_call" | custom-call | tf_op jit(solution)/shard_map/pallas_call | solution.py:361
  15.2 0.0 copy-done
  15.2 1.5 %mul.3 = f32[2,96,128]{2,1,0:T(8,128)} multiply(f32[2,96,128]{2,1,0:T(8,128)} %shard_map.55, f32[2,96,128]{2,1,0:T(8,128)S(1)} %copy-done) | non-fusion elementwise | flops 24576 | bytes 294912 | tf_op jit(solution)/shard_map/mul | solution.py:361
Async XLA Ops:
  0.0 15.2 %copy-start = (f32[2,96,128]{2,1,0:T(8,128)S(1)}, f32[2,96,128]{2,1,0:T(8,128)}, u32[]{:S(2)}) copy-start(f32[2,96,128]{2,1,0:T(8,128)} %norm_hbm.1) | copy-start | bytes 294916
